TPU v7x, 1024 devices: a whole 4x8x16 slice. The times are simulated.
1024 devices in a mesh: layer: 4 (over x), row: 16 (over y, core), col: 16 (over z).
Axes of the slice: x: 4, y: 8, z: 16, core: 2. Of those that a mesh axis runs over, the one named last changes fastest.
Arguments:
- partials: float32 [4, 1, 16, 256, 1, 16, 256], P('layer', None, 'row', None, None, 'col'), as said below
- pattern: int32 [1, 16, 2, 1, 16, 2], P(None, 'row', None, None, 'col'), may hold values from 0 to 1, as said below
Outputs:
- schur: float32 [1, 16, 4, 64, 1, 16, 256], P(None, 'row', 'layer', None, None, 'col')
- factor_panels: float32 [2, 1, 16, 256, 256], P(None, None, 'row')
Inputs may be any that keep to these rules, and one draw needn't show every extreme that they name: `partials`: each layer's partial is symmetric; in their sum the leading principal submatrix of order 2 * 256 is positive definite. `pattern`: symmetric in the global tile index.
All inputs are finite; a program needn't handle non-finite values.
Results may differ from a plain program's by a relative error of at most 0.0001.
Values sent between devices are 32-bit elements; how exact they have to be, the bound alone decides.
A program may use at most 32 MiB of HBM per device.

v0:
```python
import jax
import jax.numpy as jnp
from jax import lax
from jax.sharding import PartitionSpec as P


def broadcast(block, axis, owner):
    block = jnp.where(lax.axis_index(axis) == owner, block, jnp.zeros_like(block))
    return lax.psum(block, axis)


def right_solve(diag_factor, block):
    return jax.scipy.linalg.solve_triangular(diag_factor, block.T, lower=True).T


def left_solve(diag_factor, block):
    return jax.scipy.linalg.solve_triangular(diag_factor, block, lower=True)


def on_device(partials, pattern):
    row_count = lax.axis_size("row")
    col_count = lax.axis_size("col")
    layer_count = lax.axis_size("layer")
    row_index = lax.axis_index("row")
    col_index = lax.axis_index("col")
    layer_index = lax.axis_index("layer")
    row_blocks = partials.shape[1]
    panel_width = partials.shape[3]
    col_blocks = partials.shape[4]
    tiles_per = pattern.shape[2]
    tile_size = panel_width // tiles_per
    slab_rows = panel_width // layer_count
    own_part = partials.reshape(row_blocks, panel_width, col_blocks, panel_width)
    front_sum = lax.psum(own_part, "layer")
    held_rows = front_sum.shape[1]
    row_ids = jnp.arange(row_blocks, dtype=jnp.int32) * row_count + row_index
    col_ids = jnp.arange(col_blocks, dtype=jnp.int32) * col_count + col_index
    tile_pattern = pattern.reshape(row_blocks, tiles_per, col_blocks, tiles_per)
    kept_tiles = (
        (tile_pattern > 0) | (row_ids[:, None, None, None] < 2) | (col_ids[None, None, :, None] < 2)
    )
    entry_keep = jnp.broadcast_to(
        kept_tiles[:, :, None, :, :, None],
        (row_blocks, tiles_per, tile_size, col_blocks, tiles_per, tile_size),
    )
    entry_keep = entry_keep.reshape(row_blocks, panel_width, col_blocks, panel_width)
    panel_list = []
    for panel in range(2):
        root_row = panel % row_count
        local_row = panel // row_count
        root_col = panel % col_count
        local_col = panel // col_count
        block_row = front_sum[local_row]
        diagonal = broadcast(
            block_row[:, local_col, :], ("row", "col"), root_row * col_count + root_col
        )
        diag_factor = jnp.linalg.cholesky(diagonal)
        rows_below = row_ids > panel
        rows_panel = row_ids == panel
        cols_below = col_ids > panel
        column_raw = front_sum[:, :, local_col, :].reshape(row_blocks * held_rows, panel_width)
        solved = right_solve(diag_factor, column_raw).reshape(row_blocks, held_rows, panel_width)
        lower_mine = jnp.where(
            rows_below[:, None, None],
            solved,
            jnp.where(rows_panel[:, None, None], diag_factor[None], 0.0),
        )
        lower_rows = broadcast(lower_mine, "col", root_col)
        row_raw = block_row.reshape(panel_width, col_blocks * panel_width)
        upper_mine = left_solve(diag_factor, row_raw).reshape(panel_width, col_blocks, panel_width)
        upper_mine = jnp.where(cols_below[None, :, None], upper_mine, 0.0)
        upper_cols = broadcast(upper_mine, "row", root_row)
        product = jnp.einsum(
            "aij,jbk->aibk",
            lower_rows,
            upper_cols,
            precision=lax.Precision.HIGHEST,
            preferred_element_type=jnp.float32,
        )
        front_sum = front_sum - jnp.where(entry_keep, product, 0.0)
        panel_list.append(lower_rows)
    stacked = jnp.stack(panel_list)
    layered = front_sum.reshape(row_blocks, layer_count, slab_rows, col_blocks, panel_width)
    own_slab = lax.dynamic_slice_in_dim(layered, layer_index, 1, 1)
    schur = own_slab.reshape(row_blocks, 1, 1, slab_rows, col_blocks, 1, panel_width)
    factor_panels = stacked.reshape(2, row_blocks, 1, panel_width, panel_width)
    return (schur, factor_panels)


def solution(mesh):
    return jax.shard_map(
        on_device,
        mesh=mesh,
        in_specs=(
            P("layer", None, "row", None, None, "col", None),
            P(None, "row", None, None, "col", None),
        ),
        out_specs=(
            P(None, "row", "layer", None, None, "col", None),
            P(None, None, "row", None, None),
        ),
        check_vma=False,
    )
```

profile of v0, /device:TPU:6, one launch (start us, length us, event | category | flops | bytes accessed | tf_op | source)
XLA Modules:
  0.0 1434.5 jit_solution(11972887449438613608)
XLA Ops:
  7.2 1.8 copy.24
  9.1 73.2 %all-reduce.9.cloned.1.call-done = f32[1,256,1,256]{1,3,2,0:T(8,128)} async-done(((f32[1,256,1,256]{1,3,2,0:T(8,128)}), f32[1,256,1,256]{1,3,2,0:T(8,128)}) %all-reduce.9.cloned.1.call-update) | async-done | bytes 262160 | tf_op jit(solution)/shard_map/psum | solution.py:34
  82.3 1.7 broadcast_select_fusion.1
  84.0 339.6 %all-reduce.11.cloned.1.call-done = f32[256,256]{0,1:T(8,128)} async-done(((f32[256,256]{0,1:T(8,128)}), f32[256,256]{0,1:T(8,128)}) %all-reduce.11.cloned.1.call-update) | async-done | bytes 262160 | tf_op jit(solution)/shard_map/psum | solution.py:9
  423.6 1.1 copy.25
  424.8 11.7 cholesky.130
  436.7 9.8 custom-call.15
  447.1 11.7 cholesky.147
  458.9 0.7 compare_reduce_fusion.2
  461.1 4.4 while.8
  461.3 0.6 fusion.59
  461.9 1.4 dynamic-slice.16
  463.4 0.6 fusion.59
  464.0 1.4 dynamic-slice.16
  465.5 19.7 %custom-call.16 = f32[2,128,128]{1,2,0:T(8,128)S(1)} custom-call(f32[2,128,128]{2,1,0:T(8,128)S(1)} %get-tuple-element.30), custom_call_target="InvertDiagBlocksLowerTriangular" | custom-call | tf_op jit(solution)/shard_map/jit(_solve_triangular)/triangular_solve | solution.py:13
  485.5 0.4 convolution_subtract_fusion.2
  486.0 0.3 fusion.25
  486.9 0.3 fusion.34
  487.2 0.7 fusion.7
  488.0 0.8 fusion.6
  488.9 0.7 copy-done.5
  489.9 119.1 %all-reduce.15.cloned.1.call-done = f32[256,256]{0,1:T(8,128)} async-done(((f32[256,256]{0,1:T(8,128)}), f32[256,256]{0,1:T(8,128)}) %all-reduce.15.cloned.1.call-update) | async-done | bytes 262160 | tf_op jit(solution)/shard_map/psum | solution.py:9
  608.9 146.1 %all-reduce.13.cloned.1.call-done = f32[1,256,256]{1,2,0:T(8,128)} async-done(((f32[1,256,256]{1,2,0:T(8,128)}), f32[1,256,256]{1,2,0:T(8,128)}) %all-reduce.13.cloned.1.call-update) | async-done | bytes 262160 | tf_op jit(solution)/shard_map/psum | solution.py:9
  755.0 2.1 broadcast_select_fusion
  757.2 334.8 %all-reduce.17.cloned.1.call-done = f32[256,256]{0,1:T(8,128)} async-done(((f32[256,256]{0,1:T(8,128)}), f32[256,256]{0,1:T(8,128)}) %all-reduce.17.cloned.1.call-update) | async-done | bytes 262160 | tf_op jit(solution)/shard_map/psum | solution.py:9
  1092.0 1.1 copy.34
  1093.2 11.7 cholesky.164
  1105.1 9.8 custom-call.18
  1115.5 11.7 cholesky.181
  1127.3 0.6 compare_reduce_fusion.1
  1128.0 0.7 compare_reduce_fusion
  1130.0 4.4 while.9
  1130.3 0.6 fusion.60
  1130.9 1.4 dynamic-slice.18
  1132.4 0.6 fusion.60
  1133.0 1.4 dynamic-slice.18
  1134.4 19.7 %custom-call.19 = f32[2,128,128]{1,2,0:T(8,128)S(1)} custom-call(f32[2,128,128]{2,1,0:T(8,128)S(1)} %get-tuple-element.32), custom_call_target="InvertDiagBlocksLowerTriangular" | custom-call | tf_op jit(solution)/shard_map/jit(_solve_triangular)/triangular_solve | solution.py:13
  1154.1 0.3 fusion.19
  1154.4 0.4 convolution_subtract_fusion
  1154.9 0.3 fusion.21
  1155.8 0.3 fusion.36
  1156.2 0.7 fusion.11
  1157.0 0.8 fusion.10
  1157.8 120.1 %all-reduce.21.cloned.1.call-done = f32[256,256]{0,1:T(8,128)} async-done(((f32[256,256]{0,1:T(8,128)}), f32[256,256]{0,1:T(8,128)}) %all-reduce.21.cloned.1.call-update) | async-done | bytes 262160 | tf_op jit(solution)/shard_map/psum | solution.py:9
  1277.9 146.2 %all-reduce.19.cloned.1.call-done = f32[1,256,256]{1,2,0:T(8,128)} async-done(((f32[1,256,256]{1,2,0:T(8,128)}), f32[1,256,256]{1,2,0:T(8,128)}) %all-reduce.19.cloned.1.call-update) | async-done | bytes 262160 | tf_op jit(solution)/shard_map/psum | solution.py:9
  1424.1 1.4 fusion.3
  1425.7 0.7 reshape.139
  1426.7 1.0 copy.44
  (82 shorter events, 5.2 us)
Async XLA Ops:
  7.2 75.1 %all-reduce.9.cloned.1.call-start = ((), (), s32[]{:S(2)}) async-start(), calls=%async_computation | async-start | bytes 524288 | tf_op jit(solution)/shard_map/psum | solution.py:34
  9.0 414.6 %all-reduce.11.cloned.1.call-start = ((), (), s32[]{:S(2)}) async-start(), calls=%async_computation.1 | async-start | bytes 524288 | tf_op jit(solution)/shard_map/psum | solution.py:9
  84.0 525.0 %all-reduce.15.cloned.1.call-start = ((), (), s32[]{:S(2)}) async-start(), calls=%async_computation.3 | async-start | bytes 524288 | tf_op jit(solution)/shard_map/psum | solution.py:9
  423.6 1.2 copy-start.2
  461.1 24.1 %copy-start = (f32[1,256,1,256]{1,3,2,0:T(8,128)S(1)}, f32[1,256,1,256]{1,3,2,0:T(8,128)}, u32[]{:S(2)}) copy-start(f32[1,256,1,256]{1,3,2,0:T(8,128)} %all-reduce.9.cloned.1.call-done) | copy-start | bytes 786436
  488.0 267.0 %all-reduce.13.cloned.1.call-start = ((), (), s32[]{:S(2)}) async-start(), calls=%async_computation.2 | async-start | bytes 524288 | tf_op jit(solution)/shard_map/psum | solution.py:9
  488.8 603.2 %all-reduce.17.cloned.1.call-start = ((), (), s32[]{:S(2)}) async-start(), calls=%async_computation.4 | async-start | bytes 524288 | tf_op jit(solution)/shard_map/psum | solution.py:9
  488.9 0.7 copy-start.5
  757.2 520.7 %all-reduce.21.cloned.1.call-start = ((), (), s32[]{:S(2)}) async-start(), calls=%async_computation.6 | async-start | bytes 524288 | tf_op jit(solution)/shard_map/psum | solution.py:9
  1092.0 1.2 copy-start.1
  1156.9 267.2 %all-reduce.19.cloned.1.call-start = ((), (), s32[]{:S(2)}) async-start(), calls=%async_computation.5 | async-start | bytes 524288 | tf_op jit(solution)/shard_map/psum | solution.py:9
  1425.5 1.0 copy-start.4
  1425.7 1.0 copy-start.3
Sparse Core Ops, SparseCore 0:
  10.9 71.3 all-reduce.8
  86.7 336.8 all-reduce.10
  488.1 120.8 all-reduce.14
  611.1 143.8 all-reduce.12
  759.3 332.6 all-reduce.16
  1157.0 120.8 all-reduce.20
  1280.2 143.8 all-reduce.18
where the time goes:
time: 1430 us
  waiting for transfers between devices  1280 us (90%)
  other arithmetic  113 us (8%)
  between operations  17.2 us (1%)
  local copies, waits for them, and re-layouts  16.3 us (1%)
    psum x6, waiting for transfers between devices, broadcast(): return lax.psum(block, axis)  1210 us
    psum x1, waiting for transfers between devices, on_device(): front_sum = lax.psum(own_part, 'layer')  73.2 us
    another operation x13, other arithmetic, on_device(): diag_factor = jnp.linalg.cholesky(diagonal)  68.7 us
    another operation x5, other arithmetic, right_solve(): return jax.scipy.linalg.solve_triangular(diag_factor, block.T, lower=True).T  39.4 us
  transfers between devices with their start and end apart: 7, of which 7 were waited for; matrix products, arithmetic and copies ran while one was open for 0% of the time, Pallas kernels for 0%

commit v1 on v0

v1 whole, which is shorter than its diff:
```python
import jax
import jax.numpy as jnp
from jax import lax
from jax.experimental import pallas as pl
from jax.experimental.pallas import tpu as pltpu
from jax.sharding import PartitionSpec as P

MESH = pl.DeviceIdType.MESH
EXACT = lax.Precision.HIGHEST
F32 = jnp.float32


def dot(a, b):
    return lax.dot_general(a, b, (((1,), (0,)), ((), ())), precision=EXACT, preferred_element_type=F32)


def dot_t(a, b):
    return lax.dot_general(a, b, (((1,), (1,)), ((), ())), precision=EXACT, preferred_element_type=F32)


def exchange(
    part, slab, prow, qcol, lead,
    xin, x_send, x_recv, z_send, z_recv, y_send, yd_send, y_recv, yd_recv,
    g_send, g_recv, w_send, w_recv,
):
    l = lax.axis_index("layer")
    r = lax.axis_index("row")
    c = lax.axis_index("col")
    core = lax.rem(r, 2)
    other = r + 1 - 2 * core
    peers = [lax.rem(l + d, 4) for d in (1, 2, 3)]
    sources = [lax.rem(l + 4 - d, 4) for d in (1, 2, 3)]

    barrier = pltpu.get_barrier_semaphore()

    def greet(device):
        pl.semaphore_signal(barrier, inc=1, device_id=device, device_id_type=MESH)

    for k in range(2):
        @pl.when(c != k)
        def _():
            greet((l, r, k))

    @pl.when(r >= 2)
    def _():
        greet((l, core, c))

    for peer in peers:
        greet((peer, r, c))
    greet((l, other, c))
    waits = 4 + jnp.where(c < 2, 15, 0) + jnp.where(r < 2, 7, 0)
    pl.semaphore_wait(barrier, waits)

    def x_copy(i, peer):
        return pltpu.make_async_remote_copy(
            src_ref=part.at[pl.ds(pl.multiple_of(peer * 64, 64), 64)],
            dst_ref=xin.at[l],
            send_sem=x_send.at[i], recv_sem=x_recv.at[i],
            device_id=(peer, r, c), device_id_type=MESH,
        )

    x_copies = [x_copy(i, peer) for i, peer in enumerate(peers)]
    for copy in x_copies:
        copy.start()
    xin[l] = part[pl.ds(pl.multiple_of(l * 64, 64), 64), :]
    for copy in x_copies:
        copy.wait_recv()
    total = (xin[0] + xin[1]) + (xin[2] + xin[3])
    slab[...] = total

    def z_copy(i, k):
        return pltpu.make_async_remote_copy(
            src_ref=slab, dst_ref=prow.at[k, l],
            send_sem=z_send.at[i], recv_sem=z_recv.at[k],
            device_id=(l, r, lax.rem(c + Z_ORDER[i], 16)), device_id_type=MESH,
        )

    for k in range(2):
        @pl.when(c == k)
        def _():
            for i in range(15):
                z_copy(i, k).start()
            prow[k, l] = total

    def y_copy(i, k):
        return pltpu.make_async_remote_copy(
            src_ref=slab, dst_ref=qcol.at[k, l],
            send_sem=y_send.at[i], recv_sem=y_recv,
            device_id=(l, lax.rem(r + 2 * Y_ORDER[i], 16), c), device_id_type=MESH,
        )

    for k in range(2):
        @pl.when(r == k)
        def _():
            for i in range(7):
                y_copy(i, k).start()
            qcol[k, l] = total

    def yd_copy(i, src, dst, s):
        return pltpu.make_async_remote_copy(
            src_ref=prow.at[src, l], dst_ref=lead.at[dst, l],
            send_sem=yd_send.at[s, i], recv_sem=yd_recv.at[s],
            device_id=(l, lax.rem(r + 2 * Y_ORDER[i], 16), c), device_id_type=MESH,
        )

    for k in range(2):
        @pl.when(c != k)
        def _():
            z_copy(0, k).wait_recv()

        for owner, dst in (((0, 0), (1, 1)) if k == 0 else ((1, 2),)):
            @pl.when(r == owner)
            def _():
                for i in range(7):
                    yd_copy(i, k, dst, k).start()
                lead[dst, l] = prow[k, l]

    @pl.when(r >= 2)
    def _():
        yd_copy(0, 0, 0, 0).wait_recv()

        @pl.when(core == 1)
        def _():
            yd_copy(0, 1, 2, 1).wait_recv()

    def g_copy(i, ref, j):
        return pltpu.make_async_remote_copy(
            src_ref=ref, dst_ref=ref,
            send_sem=g_send.at[j, i], recv_sem=g_recv.at[j, i],
            device_id=(peers[i], r, c), device_id_type=MESH,
        )

    def g_all(ref, j):
        return [g_copy(i, ref, j) for i in range(3)]

    lead_of = ((0,), (1, 2))
    for k in range(2):
        @pl.when(core == k)
        def _():
            for j, b in enumerate(lead_of[k]):
                for copy in g_all(lead.at[b, l], j):
                    copy.start()
    for k in range(2):
        for copy in g_all(prow.at[k, l], 2 + k):
            copy.start()

    @pl.when(r >= 2)
    def _():
        y_copy(0, 0).wait_recv()

    for k in range(2):
        @pl.when(core == k)
        def _():
            for copy in g_all(qcol.at[k, l], 4):
                copy.start()

    def w_copy(ref, j):
        return pltpu.make_async_remote_copy(
            src_ref=ref, dst_ref=ref, send_sem=w_send.at[j], recv_sem=w_recv.at[j],
            device_id=(l, other, c), device_id_type=MESH,
        )

    for k in range(2):
        @pl.when(core == k)
        def _():
            for j, b in enumerate(lead_of[k]):
                for copy in g_all(lead.at[b, l], j):
                    copy.wait_recv()
                w_copy(lead.at[b], j).start()
            for copy in g_all(qcol.at[k, l], 4):
                copy.wait_recv()
            w_copy(qcol.at[k], 2).start()
    for k in range(2):
        for copy in g_all(prow.at[k, l], 2 + k):
            copy.wait_recv()
    for k in range(2):
        @pl.when(core == k)
        def _():
            for j, b in enumerate(lead_of[1 - k]):
                w_copy(lead.at[b], j).wait_recv()
            w_copy(qcol.at[1 - k], 2).wait_recv()
            for j, b in enumerate(lead_of[k]):
                for copy in g_all(lead.at[b, l], j):
                    copy.wait_send()
                w_copy(lead.at[b], j).wait_send()
            for copy in g_all(qcol.at[k, l], 4):
                copy.wait_send()
            w_copy(qcol.at[k], 2).wait_send()
    for k in range(2):
        for copy in g_all(prow.at[k, l], 2 + k):
            copy.wait_send()
    for copy in x_copies:
        copy.wait_send()

    @pl.when(c < 2)
    def _():
        for i in range(15):
            z_copy(i, 0).wait_send()

    @pl.when(r < 2)
    def _():
        for i in range(7):
            y_copy(i, 0).wait_send()
            yd_copy(i, 0, 0, 0).wait_send()

    @pl.when(r == 1)
    def _():
        for i in range(7):
            yd_copy(i, 1, 2, 1).wait_send()


Z_ORDER = (8, 7, 9, 6, 10, 5, 11, 4, 12, 3, 13, 2, 14, 1, 15)
Y_ORDER = (4, 3, 5, 2, 6, 1, 7)


def lanes(x, k):
    return jnp.broadcast_to(x[:, k : k + 1], (8, 128))


def rows(x, k):
    return jnp.broadcast_to(x[k : k + 1, :], (8, 128))


def factor_tile(tile):
    lane = lax.broadcasted_iota(jnp.int32, (8, 128), 1)
    sub = lax.broadcasted_iota(jnp.int32, (8, 128), 0)
    x = [tile[8 * g : 8 * g + 8, :] for g in range(16)]
    upper, inverse = [], []
    for b in range(16):
        base = 8 * b
        y = x[b]
        cols = [lanes(y, base + k) for k in range(8)]
        z = jnp.where(lane < base, y, jnp.where(lane == base + sub, 1.0, 0.0))
        entry = {}
        recip = []
        pivots = None
        for j in range(8):
            d = rows(cols[j], j)
            pivots = d if pivots is None else jnp.where(sub >= j, d, pivots)
            recip.append(1.0 / d)
            if j < 7:
                m = jnp.where(sub > j, cols[j], 0.0) * recip[j]
                for k in range(j + 1, 8):
                    entry[j, k] = rows(cols[k], j)
                    cols[k] = cols[k] - m * entry[j, k]
                y = y - m * rows(y, j)
                z = z - m * rows(z, j)
        scale = lax.rsqrt(pivots)
        upper.append(jnp.where(lane >= base + sub, y * scale, 0.0))
        inverse.append(z * scale)
        if b < 15:
            v = jnp.where(lane < base + 8, z, y)
            v_rows = [rows(v, j) for j in range(8)]
            inside = (lane >= base) & (lane < base + 8)
            for g in range(b + 1, 16):
                cg = [lanes(x[g], base + k) for k in range(8)]
                acc = jnp.where(inside, 0.0, x[g])
                for j in range(8):
                    m = cg[j] * recip[j]
                    for k in range(j + 1, 8):
                        cg[k] = cg[k] - m * entry[j, k]
                    acc = acc - m * v_rows[j]
                x[g] = acc
    return jnp.concatenate(upper, axis=0), jnp.concatenate(inverse, axis=0)


def factor_block(block):
    upper0, g0 = factor_tile(block[:128, :128])
    low = dot_t(block[128:, :128], g0)
    upper1, g1 = factor_tile(block[128:, 128:] - dot_t(low, low))
    zero = jnp.zeros((128, 128), F32)
    factor = jnp.concatenate(
        [jnp.concatenate([upper0.T, zero], axis=1), jnp.concatenate([low, upper1.T], axis=1)], axis=0
    )
    corner = -dot(g1, dot(low, g0))
    inverse = jnp.concatenate(
        [jnp.concatenate([g0, zero], axis=1), jnp.concatenate([corner, g1], axis=1)], axis=0
    )
    return factor, inverse


def eliminate(pattern, slab, prow, qcol, lead, schur, panels):
    l = lax.axis_index("layer")
    r = lax.axis_index("row")
    c = lax.axis_index("col")
    a00, a10, a11 = (lead[i].reshape(256, 256) for i in range(3))
    p0, p1 = (prow[i].reshape(256, 256) for i in range(2))
    q0, q1 = (qcol[i].reshape(256, 256) for i in range(2))
    f0, inv0 = factor_block(a00)
    l10 = dot_t(a10, inv0)
    rest = a11 - dot_t(l10, l10)
    l0 = jnp.where(r == 0, f0, dot_t(p0, inv0))
    u0 = dot(inv0, q0)
    p1 = p1 - dot_t(l0, l10)
    q1 = q1 - dot(l10, u0)
    u0 = jnp.where(c == 0, 0.0, u0)
    panels[0] = l0
    f1, inv1 = factor_block(rest)
    l1 = jnp.where(r == 0, 0.0, jnp.where(r == 1, f1, dot_t(p1, inv1)))
    u1 = jnp.where(c < 2, 0.0, dot(inv1, q1))
    panels[1] = l1
    mine = pl.ds(pl.multiple_of(l * 64, 64), 64)
    product = dot(panels[0, mine, :], u0) + dot(panels[1, mine, :], u1)
    half = lax.div(l, 2)
    lane = lax.broadcasted_iota(jnp.int32, (64, 256), 1)
    flag = jnp.where(lane < 128, pattern[half, 0], pattern[half, 1])
    keep = (flag > 0) | (r < 2) | (c < 2)
    schur[...] = slab[...] - jnp.where(keep, product, 0.0)


def on_device(partials, pattern):
    vmem = pl.BlockSpec(memory_space=pltpu.VMEM)
    dma = pltpu.SemaphoreType.DMA
    slab, prow, qcol, lead = pl.pallas_call(
        exchange,
        out_shape=[
            jax.ShapeDtypeStruct((64, 256), F32),
            jax.ShapeDtypeStruct((2, 4, 64, 256), F32),
            jax.ShapeDtypeStruct((2, 4, 64, 256), F32),
            jax.ShapeDtypeStruct((3, 4, 64, 256), F32),
        ],
        in_specs=[vmem],
        out_specs=[vmem] * 4,
        scratch_shapes=[
            pltpu.VMEM((4, 64, 256), F32),
            dma((3,)), dma((3,)), dma((15,)), dma((2,)), dma((7,)), dma((2, 7)), dma, dma((2,)),
            dma((5, 3)), dma((5, 3)), dma((3,)), dma((3,)),
        ],
        compiler_params=pltpu.CompilerParams(
            collective_id=0, has_side_effects=True, vmem_limit_bytes=32 * 1024 * 1024
        ),
        name="exchange",
    )(partials.reshape(256, 256))
    schur, panels = pl.pallas_call(
        eliminate,
        out_shape=[
            jax.ShapeDtypeStruct((64, 256), F32),
            jax.ShapeDtypeStruct((2, 256, 256), F32),
        ],
        in_specs=[pl.BlockSpec(memory_space=pltpu.SMEM)] + [vmem] * 4,
        out_specs=[vmem] * 2,
        compiler_params=pltpu.CompilerParams(vmem_limit_bytes=32 * 1024 * 1024),
        name="eliminate",
    )(pattern.reshape(2, 2), slab, prow, qcol, lead)
    return schur.reshape(1, 1, 1, 64, 1, 1, 256), panels.reshape(2, 1, 1, 256, 256)


def solution(mesh):
    return jax.shard_map(
        on_device,
        mesh=mesh,
        in_specs=(
            P("layer", None, "row", None, None, "col", None),
            P(None, "row", None, None, "col", None),
        ),
        out_specs=(
            P(None, "row", "layer", None, None, "col", None),
            P(None, None, "row", None, None),
        ),
        check_vma=False,
    )
```

time: 1430 us -> 84.2 us (0.06)
  the two profiles are of different devices: /device:TPU:6 before, /device:TPU:177 now
where the time goes in v1:
time: 84.2 us; the launch traced here: 84 us
  Pallas kernels  81 us (96%)
  local copies, waits for them, and re-layouts  2.34 us (3%)
    pallas_call x1, Pallas kernels, on_device(): pl.pallas_call(exchange, out_shape=[jax.ShapeDtypeStruct((64, 256), F32),...  60.1 us
    pallas_call x1, Pallas kernels, on_device(): pl.pallas_call(eliminate, out_shape=[jax.ShapeDtypeStruct((64, 256), F32)...  20.9 us
    unnamed x4, local copies, waits for them, and re-layouts  2.34 us

profile of v1, /device:TPU:177, one launch (start us, length us, event | category | flops | bytes accessed | tf_op | source)
XLA Modules:
  0.0 84.0 jit_solution(16675369837833759625)
XLA Ops:
  0.6 1.0 %copy.8 = f32[1,1,1,256,1,1,256]{6,3,4,5,2,1,0:T(8,128)S(1)} copy(f32[1,1,1,256,1,1,256]{6,5,4,3,2,1,0:T(1,128)} %param.2) | data formatting | bytes 524288
  1.6 60.1 %exchange.1 = (f32[64,256]{1,0:T(8,128)S(1)}, f32[2,4,64,256]{3,2,1,0:T(8,128)S(1)}, f32[2,4,64,256]{3,2,1,0:T(8,128)S(1)}, f32[3,4,64,256]{3,2,1,0:T(8,128)S(1)}) custom-call(f32[256,256]{1,0:T(8,128)S(1)} %bitcast.8), custom_call_target="tpu_custom_call" | custom-call | tf_op jit(solution)/shard_map/exchange/pallas_call | solution.py:314
  61.7 0.0 copy-start
  61.7 0.7 copy-done
  62.4 20.9 %eliminate.1 = (f32[64,256]{1,0:T(8,128)S(1)}, f32[2,256,256]{2,1,0:T(8,128)}) custom-call(s32[2,2]{1,0:T(2,128)S(1)} %bitcast.10, f32[64,256]{1,0:T(8,128)S(1)} %get-tuple-element.8.slab, f32[2,4,64,256]{3,2,1,0:T(8,128)S(1)} %get-tuple-element.9.prow, f32[2,4,64,256]{3,2,1,0:T(8,128)S(1)} %get-tuple-element.10.qcol, ...), custom_call_target="tpu_custom_call" | custom-call | tf_op jit(solution)/shard_map/eliminate/pallas_call | solution.py:334
  83.3 0.7 copy.4
Async XLA Ops:
  61.7 0.7 copy-start

commit v2 on v0

v2 whole, which is shorter than its diff:
```python
import jax
import jax.numpy as jnp
from jax import lax
from jax.experimental import pallas as pl
from jax.experimental.pallas import tpu as pltpu
from jax.sharding import PartitionSpec as P

MESH = pl.DeviceIdType.MESH
EXACT = lax.Precision.HIGHEST
F32 = jnp.float32


def dot(a, b):
    return lax.dot_general(a, b, (((1,), (0,)), ((), ())), precision=EXACT, preferred_element_type=F32)


def dot_t(a, b):
    return lax.dot_general(a, b, (((1,), (1,)), ((), ())), precision=EXACT, preferred_element_type=F32)


def lanes(x, k):
    return jnp.broadcast_to(x[:, k : k + 1], (8, 128))


def rows(x, k):
    return jnp.broadcast_to(x[k : k + 1, :], (8, 128))


def factor_tile(tile):
    lane=lax.broadcasted_iota(jnp.int32,(8,128),1); sub=lax.broadcasted_iota(jnp.int32,(8,128),0)
    X=[tile[8*g:8*g+8,:] for g in range(16)]; FT=[];G=[]
    for b in range(0,16,2):
        base=8*b
        Y0,Y1=X[b],X[b+1]
        c0=[lanes(Y0,base+k) for k in range(8)]
        c1=[lanes(Y1,base+k) for k in range(16)]
        Z0=jnp.where(lane<base,Y0,jnp.where(lane==base+sub,1.0,0.0))
        Z1=jnp.where(lane<base,Y1,jnp.where(lane==base+8+sub,1.0,0.0))
        U={};p=[]; dv=[None,None]; pv=[None,None]
        d=rows(c0[0],0)
        for j in range(16):
            h,q=divmod(j,8)
            dv[h]=d if q==0 else jnp.where(sub>=q,d,dv[h])
            pj=1.0/d; p.append(pj)
            pv[h]=pj if q==0 else jnp.where(sub>=q,pj,pv[h])
            if j==15: break
            if h==0:
                if j<7: e1=rows(c0[j+1],j); dn=rows(c0[j+1],j+1)
                else: e1=rows(c1[j],0); dn=rows(c1[8],0)
                d=dn-(e1*pj)*e1
                m0=jnp.where(sub>j,c0[j],0.0)*pj if j<7 else None
                m1=c1[j]*pj
                for k in range(j+1,8):
                    u=rows(c0[k],j); U[j,k]=u
                    c0[k]=c0[k]-m0*u; c1[k]=c1[k]-m1*u
                for k in range(8,16):
                    u=rows(c1[j],k-8); U[j,k]=u
                    c1[k]=c1[k]-m1*u
                y=rows(Y0,j); z=rows(Z0,j)
                if j<7: Y0=Y0-m0*y; Z0=Z0-m0*z
                Y1=Y1-m1*y; Z1=Z1-m1*z
            else:
                e1=rows(c1[j+1],q); d=rows(c1[j+1],q+1)-(e1*pj)*e1
                m1=jnp.where(sub>q,c1[j],0.0)*pj
                for k in range(j+1,16):
                    u=rows(c1[k],q); U[j,k]=u
                    c1[k]=c1[k]-m1*u
                Y1=Y1-m1*rows(Y1,q); Z1=Z1-m1*rows(Z1,q)
        for h,(Y,Z) in enumerate(((Y0,Z0),(Y1,Z1))):
            rs=lax.rsqrt(dv[h])
            FT.append(jnp.where(lane>=base+8*h+sub,Y*rs,0.0)); G.append(Z*rs)
        if b<14:
            V0=jnp.where(lane<base+16,Z0,Y0); V1=jnp.where(lane<base+16,Z1,Y1)
            inb=(lane>=base)&(lane<base+16)
            for g in (b+2,b+3):
                cg=[lanes(X[g],base+k) for k in range(16)]
                acc=jnp.where(inb,0.0,X[g])
                for j in range(16):
                    m=cg[j]*p[j]
                    for k in range(j+1,16): cg[k]=cg[k]-m*U[j,k]
                    acc=acc-m*rows(V0 if j<8 else V1,j%8)
                X[g]=acc
            if b<12:
                K0=V0*pv[0]; K1=V1*pv[1]
                for j in range(15,0,-1):
                    h,q=divmod(j,8)
                    if h==1:
                        kr=rows(K1,q)
                        if q>0: K1=K1-jnp.where(sub<q,c1[j]*pv[1],0.0)*kr
                        col=U[0,j]
                        for i in range(1,8): col=jnp.where(sub>=i,U[i,j],col)
                        K0=K0-col*pv[0]*kr
                    else:
                        K0=K0-jnp.where(sub<q,c0[j]*pv[0],0.0)*rows(K0,q)
                Kr=[rows(K0,j) for j in range(8)]+[rows(K1,j) for j in range(8)]
                for g in range(b+4,16):
                    acc=jnp.where(inb,0.0,X[g])
                    for j in range(16): acc=acc-lanes(X[g],base+j)*Kr[j]
                    X[g]=acc
    return jnp.concatenate(FT,axis=0), jnp.concatenate(G,axis=0)


TREE = (
    {0: (1, 2, 5, 8, 15, 13), 2: (3, 4), 5: (6, 7), 8: (9, 10), 15: (14,), 13: (12, 11)},
    {1: (0, 2, 3, 6, 9, 14, 12), 3: (4, 5), 6: (7, 8), 9: (10,), 14: (15, 13), 12: (11,)},
)
COL_ORDER = (tuple(range(1, 16)), (0,) + tuple(range(2, 16)))
CHIP_ORDER = (4, 3, 5, 2, 6, 1, 7)
HOME = ((0, 0), (1, 0), (1, 1))
CORE = (0, 1, 0)
OWNERS = ((1, 2, 3), (0, 1, 2, 3), (0, 1, 2, 3))
THIRDS = {1: (0, 48), 2: (48, 88), 3: (88, 128)}
TILES = ((0, 0), (128, 0), (128, 128))
PARTS = ((0, 0), (0, 1), (0, 2), (1, 0), (2, 0))
FIRST = (0, 1, 2)
SECOND, THIRD = 3, 4


def parent_col(k, c):
    up = jnp.int32(0)
    for sender, cols in TREE[k].items():
        for col in cols:
            up = jnp.where(c == col, sender, up)
    return up


def piece(ref, p, owner):
    b, t = PARTS[p]
    if b == 0:
        lo, hi = THIRDS[owner]
        top, left = TILES[t]
        return ref.at[0, top + lo : top + hi, left : left + 128]
    if b == 2 and owner < 2:
        return ref.at[2, 64 * owner : 64 * owner + 64, 0:128]
    return ref.at[b, 64 * owner : 64 * owner + 64]


def kernel(
    pattern, part, schur, panels,
    xin, din, slab, prow, qcol, lead, work,
    ready_y, ready_z, ready_w, x_send, x_recv, d_send, d_recv, z_send, zn_send, z_recv, y_send, y_recv,
    zd_send, zd_recv, yd_send, yd_recv, gd_send, gd_recv, g_send, g_recv,
    w_send, w_recv, wq_send, wq_recv,
):
    l = lax.axis_index("layer")
    r = lax.axis_index("row")
    c = lax.axis_index("col")
    core = lax.rem(r, 2)
    sibling = r + 1 - 2 * core
    peers = [lax.rem(l + d, 4) for d in (1, 2, 3)]
    far_row = r >= 2
    row_role = [(l > 0) | (c > 0), c >= 0]
    col_role = [(l > 0) | (r > 0), r > 0]

    def remote(src, dst, send, recv, device):
        return pltpu.make_async_remote_copy(
            src_ref=src, dst_ref=dst, send_sem=send, recv_sem=recv, device_id=device, device_id_type=MESH
        )

    barrier = pltpu.get_barrier_semaphore()

    def greet(device):
        pl.semaphore_signal(barrier, inc=1, device_id=device, device_id_type=MESH)

    for peer in peers:
        greet((peer, r, c))

    @pl.when(core == 1)
    def _():
        greet((l, sibling, c))

    for k in range(2):
        @pl.when((c == k) & col_role[k] & jnp.logical_not(far_row))
        def _():
            for col in COL_ORDER[k]:
                greet((l, r, col))

        for sender, cols in TREE[k].items():
            @pl.when((c == sender) & far_row)
            def _():
                for col in cols:
                    greet((l, r, col))

        @pl.when((r == k) & row_role[k])
        def _():
            for y in CHIP_ORDER:
                greet((l, 2 * y + k, c))
                if k == 1:
                    greet((l, 2 * y, c))

    served_y = [far_row & row_role[0] & (core == 0), far_row & row_role[1]]
    served_z = [col_role[k] & (c != k) for k in range(2)]
    count = 3
    for flag in served_y + served_z + [core == 0]:
        count = count + jnp.where(flag, 1, 0)
    pl.semaphore_wait(barrier, count)

    def ready(sem, device):
        pl.semaphore_signal(sem, inc=1, device_id=device, device_id_type=MESH)

    for k in range(2):
        @pl.when(served_y[k])
        def _():
            ready(ready_y, (l, k, c))

        @pl.when(served_z[k])
        def _():
            ready(ready_z.at[c], (l, r, jnp.where(far_row, parent_col(k, c), k)))

    @pl.when(core == 0)
    def _():
        ready(ready_w, (l, sibling, c))

    def d_copy(owner, t):
        return remote(piece(part, t, owner), piece(din.at[l], t, owner), d_send.at[owner - 1, t], d_recv.at[t, l],
                      (owner, r, c))

    def x_copy(i):
        rows_to = pl.ds(pl.multiple_of(peers[i] * 64, 64), 64)
        return remote(part.at[0, rows_to], xin.at[l], x_send.at[i], x_recv.at[i], (peers[i], r, c))

    first = (r == 0) & (c == 0)

    @pl.when(first)
    def _():
        for t in FIRST:
            for owner in OWNERS[0]:
                @pl.when(l != owner)
                def _():
                    d_copy(owner, t).start()

    for i in range(3):
        x_copy(i).start()

    own_rows = pl.ds(pl.multiple_of(l * 64, 64), 64)
    xin[l] = part[0, own_rows]

    def yd_rows(p):
        rows_to = [2 * y + CORE[PARTS[p][0]] for y in CHIP_ORDER]
        return rows_to + [0] if p == THIRD else rows_to

    def yd_copies(p, owner):
        ref = piece(lead, p, owner)
        return [
            remote(ref, ref, yd_send.at[p, i], yd_recv.at[p], (l, row, c)) for i, row in enumerate(yd_rows(p))
        ]

    def zd_copies(p, owner):
        ref = piece(lead, p, owner)
        return [
            remote(ref, ref, zd_send.at[p, i], zd_recv.at[p], (l, r, col))
            for i, col in enumerate(COL_ORDER[HOME[PARTS[p][0]][1]])
        ]

    def gd_copies(p, owner):
        ref = piece(lead, p, owner)
        return [remote(ref, ref, gd_send.at[p, i], gd_recv.at[p, owner], (peers[i], r, c)) for i in range(3)]

    def w_copy(p, owner):
        ref = piece(lead, p, owner)
        return remote(ref, ref, w_send.at[p, owner], w_recv.at[p, owner], (l, sibling, c))

    def row_sends(p, owner):
        for row, copy in zip(yd_rows(p), yd_copies(p, owner)):
            if row == 0:
                pl.semaphore_wait(ready_w, 1)
            copy.start()

    def col_sends(p, owner, wait):
        for col, copy in zip(COL_ORDER[HOME[PARTS[p][0]][1]], zd_copies(p, owner)):
            if wait:
                pl.semaphore_wait(ready_z.at[col], 1)
            copy.start()

    for k in range(2):
        @pl.when((r == k) & row_role[k])
        def _():
            pl.semaphore_wait(ready_y, (7, 14)[k])

    def add_first():
        for owner in OWNERS[0]:
            lo, hi = THIRDS[owner]

            @pl.when(first & (l == owner))
            def _():
                for t in FIRST:
                    top, left = TILES[t]
                    total = None
                    for q in range(4):
                        if q != owner:
                            remote(piece(part, t, owner), piece(din.at[q], t, owner), d_send.at[0, t],
                                   d_recv.at[t, q], (q, r, c)).wait_recv()
                        source = part if q == owner else din.at[q]
                        term = source[0, top + lo : top + hi, left : left + 128]
                        total = term if total is None else total + term
                    lead[0, top + lo : top + hi, left : left + 128] = total
                    row_sends(t, owner)
                    col_sends(t, owner, t == 0)

    def add_slab():
        for i in range(3):
            x_copy(i).wait_recv()
        slab[...] = (xin[0] + xin[1]) + (xin[2] + xin[3])

    @pl.when(first & (l > 0))
    def _():
        add_first()

    add_slab()

    def z_copies(k):
        return {
            sender: [
                remote(slab if sender == k else prow.at[k, l], prow.at[k, l],
                       z_send.at[i] if sender == k else zn_send.at[i], z_recv.at[k], (l, r, col))
                for i, col in enumerate(cols)
            ]
            for sender, cols in TREE[k].items()
        }

    def y_copies(k):
        return [
            remote(slab, qcol.at[k, l], y_send.at[i], y_recv, (l, 2 * y + k, c)) for i, y in enumerate(CHIP_ORDER)
        ]

    for p in (SECOND, THIRD):
        b = PARTS[p][0]

        @pl.when((r == 1) & (c == HOME[b][1]))
        def _():
            lead[b, own_rows] = slab[...]
            for owner in OWNERS[b]:
                @pl.when(l == owner)
                def _():
                    row_sends(p, owner)
                    col_sends(p, owner, True)

    for k in range(2):
        @pl.when((c > 0) & (r == k))
        def _():
            qcol[k, l] = slab[...]
            for copy in y_copies(k):
                copy.start()

        @pl.when(far_row & (c == k))
        def _():
            prow[k, l] = slab[...]

    for k in (1, 0):
        for sender, cols in TREE[k].items():
            @pl.when(far_row & (c == sender))
            def _():
                copies = z_copies(k)[sender]
                if sender != k:
                    copies[0].wait_recv()
                for col, copy in zip(cols, copies):
                    pl.semaphore_wait(ready_z.at[col], 1)
                    copy.start()

    for p in (SECOND, THIRD) + FIRST:
        b = PARTS[p][0]

        @pl.when((r == HOME[b][0]) & (c != HOME[b][1]))
        def _():
            for owner in OWNERS[b]:
                @pl.when(l == owner)
                def _():
                    zd_copies(p, owner)[0].wait_recv()
                    row_sends(p, owner)

    def g_copies(ref, j):
        return [remote(ref, ref, g_send.at[j, i], g_recv.at[j, i], (peers[i], r, c)) for i in range(3)]

    def gather_panels():
        @pl.when(far_row)
        def _():
            for k in range(2):
                leaf = c != k
                for sender in TREE[k]:
                    leaf = leaf & (c != sender)

                @pl.when(leaf)
                def _():
                    z_copies(k)[k][0].wait_recv()

                for copy in g_copies(prow.at[k, l], k):
                    copy.start()

        for k in range(2):
            @pl.when((c > 0) & (core == k))
            def _():
                @pl.when(far_row)
                def _():
                    y_copies(k)[0].wait_recv()

                for copy in g_copies(qcol.at[k, l], 2):
                    copy.start()

    def gather_lead(p):
        b = PARTS[p][0]

        @pl.when(core == CORE[b])
        def _():
            for owner in OWNERS[b]:
                @pl.when(l == owner)
                def _():
                    @pl.when(far_row if b < 2 else r >= 0)
                    def _():
                        yd_copies(p, owner)[0].wait_recv()

                    for copy in gd_copies(p, owner):
                        copy.start()

    def passes(p, owner):
        return (far_row | (l != owner)) if p == THIRD else (l >= 0)

    def lead_pass(p, owner):
        b = PARTS[p][0]

        @pl.when(core == CORE[b])
        def _():
            @pl.when(l != owner)
            def _():
                gd_copies(p, owner)[0].wait_recv()

            @pl.when(passes(p, owner))
            def _():
                w_copy(p, owner).start()

    def lead_wait(p, owner):
        @pl.when((core != CORE[PARTS[p][0]]) & passes(p, owner))
        def _():
            w_copy(p, owner).wait_recv()

    def wq_copy(k):
        return remote(qcol.at[k], qcol.at[k], wq_send, wq_recv, (l, sibling, c))

    def panels_pass():
        for k in range(2):
            @pl.when((c > 0) & (core == k))
            def _():
                for copy in g_copies(qcol.at[k, l], 2):
                    copy.wait_recv()
                wq_copy(k).start()

    def panels_wait():
        @pl.when(far_row)
        def _():
            for k in range(2):
                for copy in g_copies(prow.at[k, l], k):
                    copy.wait_recv()

        for k in range(2):
            @pl.when((c > 0) & (core != k))
            def _():
                wq_copy(k).wait_recv()

    @pl.when(jnp.logical_not(far_row))
    def _():
        prow[...] = jnp.zeros_like(prow)

    @pl.when(c == 0)
    def _():
        qcol[...] = jnp.zeros_like(qcol)

    @pl.when((core == 1) & far_row)
    def _():
        pl.semaphore_wait(ready_w, 1)

    gather_panels()
    gather_lead(SECOND)
    gather_lead(THIRD)
    for p in FIRST:
        gather_lead(p)

    zero = jnp.zeros((128, 128), F32)

    def finish(upper0, g0, second, ref):
        low = dot_t(second[:, :128], g0)
        upper1, g1 = factor_tile(second[:, 128:] - dot_t(low, low))
        ref[0, 0:128, 0:128] = upper0.T
        ref[0, 0:128, 128:256] = zero
        ref[0, 128:256, 0:128] = low
        ref[0, 128:256, 128:256] = upper1.T
        ref[1, 0:128, 0:128] = g0
        ref[1, 0:128, 128:256] = zero
        ref[1, 128:256, 0:128] = -dot(g1, dot(low, g0))
        ref[1, 128:256, 128:256] = g1

    for owner in OWNERS[0]:
        lead_pass(0, owner)
    for owner in OWNERS[0]:
        lead_wait(0, owner)
    upper0, g0 = factor_tile(lead[0, 0:128, 0:128])
    for p in (1, 2):
        for owner in OWNERS[0]:
            lead_pass(p, owner)
    for p in (SECOND, THIRD):
        for owner in OWNERS[1]:
            lead_pass(p, owner)
    for p in (1, 2):
        for owner in OWNERS[0]:
            lead_wait(p, owner)
    finish(upper0, g0, lead[0, 128:256, :], work)
    panels_pass()
    for p in (SECOND, THIRD):
        for owner in OWNERS[1]:
            lead_wait(p, owner)
    inv0 = work[1]
    l10 = dot_t(lead[1], inv0)
    rest = lead[2] - dot_t(l10, l10)
    work[2] = l10
    panels_wait()
    l0 = jnp.where(r == 0, work[0], jnp.where(r == 1, work[2], dot_t(prow[0].reshape(256, 256), work[1])))
    panels[0] = l0
    panels[1] = prow[1].reshape(256, 256) - dot_t(l0, work[2])
    work[5] = dot(work[1], qcol[0].reshape(256, 256))
    work[6] = qcol[1].reshape(256, 256) - dot(work[2], work[5])

    upper0, g0 = factor_tile(rest[:128, :128])
    finish(upper0, g0, rest[128:, :], work.at[3:5])

    inv1 = work[4]
    panels[1] = jnp.where(r == 0, 0.0, jnp.where(r == 1, work[3], dot_t(panels[1], inv1)))
    u1 = jnp.where(c < 2, 0.0, dot(inv1, work[6]))
    u0 = jnp.where(c == 0, 0.0, work[5])
    mine = pl.ds(pl.multiple_of(l * 64, 64), 64)
    product = dot(panels[0, mine, :], u0) + dot(panels[1, mine, :], u1)
    half = lax.div(l, 2)
    lane = lax.broadcasted_iota(jnp.int32, (64, 256), 1)
    flag = jnp.where(lane < 128, pattern[half, 0], pattern[half, 1])
    keep = (flag > 0) | (r < 2) | (c < 2)
    schur[...] = slab[...] - jnp.where(keep, product, 0.0)

    for i in range(3):
        x_copy(i).wait_send()

    @pl.when(first)
    def _():
        for t in FIRST:
            for owner in OWNERS[0]:
                @pl.when(l != owner)
                def _():
                    d_copy(owner, t).wait_send()

    for p in range(5):
        b = PARTS[p][0]
        for owner in OWNERS[b]:
            @pl.when((l == owner) & (r == HOME[b][0]))
            def _():
                @pl.when(c == HOME[b][1])
                def _():
                    for copy in zd_copies(p, owner):
                        copy.wait_send()

                for copy in yd_copies(p, owner):
                    copy.wait_send()

            @pl.when(core == CORE[b])
            def _():
                @pl.when(l == owner)
                def _():
                    for copy in gd_copies(p, owner):
                        copy.wait_send()

                @pl.when(passes(p, owner))
                def _():
                    w_copy(p, owner).wait_send()

    @pl.when(far_row)
    def _():
        for k in range(2):
            for sender in TREE[k]:
                @pl.when(c == sender)
                def _():
                    for copy in z_copies(k)[sender]:
                        copy.wait_send()

            for copy in g_copies(prow.at[k, l], k):
                copy.wait_send()

    @pl.when(c > 0)
    def _():
        @pl.when(r < 2)
        def _():
            for copy in y_copies(0):
                copy.wait_send()

        for k in range(2):
            @pl.when(core == k)
            def _():
                for copy in g_copies(qcol.at[k, l], 2):
                    copy.wait_send()
                wq_copy(k).wait_send()


def on_device(partials, pattern):
    vmem = pl.BlockSpec(memory_space=pltpu.VMEM)
    dma = pltpu.SemaphoreType.DMA
    regular = pltpu.SemaphoreType.REGULAR
    schur, panels = pl.pallas_call(
        kernel,
        out_shape=[
            jax.ShapeDtypeStruct((64, 256), F32),
            jax.ShapeDtypeStruct((2, 256, 256), F32),
        ],
        in_specs=[pl.BlockSpec(memory_space=pltpu.SMEM), vmem],
        out_specs=[vmem] * 2,
        scratch_shapes=[
            pltpu.VMEM((4, 64, 256), F32), pltpu.VMEM((4, 1, 256, 256), F32), pltpu.VMEM((64, 256), F32),
            pltpu.VMEM((2, 4, 64, 256), F32), pltpu.VMEM((2, 4, 64, 256), F32), pltpu.VMEM((3, 256, 256), F32),
            pltpu.VMEM((7, 256, 256), F32),
            regular, regular((16,)), regular,
            dma((3,)), dma((3,)), dma((3, 3)), dma((3, 4)), dma((7,)), dma((2,)), dma((2,)), dma((7,)), dma,
            dma((5, 15)), dma((5,)), dma((5, 8)), dma((5,)), dma((5, 3)), dma((5, 4)), dma((3, 3)), dma((3, 3)),
            dma((5, 4)), dma((5, 4)), dma, dma,
        ],
        compiler_params=pltpu.CompilerParams(
            collective_id=0, has_side_effects=True, vmem_limit_bytes=32 * 1024 * 1024
        ),
        name="panels",
    )(pattern.reshape(2, 2), partials.reshape(1, 256, 256))
    return schur.reshape(1, 1, 1, 64, 1, 1, 256), panels.reshape(2, 1, 1, 256, 256)


def solution(mesh):
    return jax.shard_map(
        on_device,
        mesh=mesh,
        in_specs=(
            P("layer", None, "row", None, None, "col", None),
            P(None, "row", None, None, "col", None),
        ),
        out_specs=(
            P(None, "row", "layer", None, None, "col", None),
            P(None, None, "row", None, None),
        ),
        check_vma=False,
    )
```

time: 1430 us -> 61.3 us (0.04)
  the two profiles are of different devices: /device:TPU:6 before, /device:TPU:905 now
where the time goes in v2:
time: 61.3 us; the launch traced here: 61.1 us
  Pallas kernels  57.3 us (93%)
  local copies, waits for them, and re-layouts  3.13 us (5%)
  between operations  0.65 us (1%)
    pallas_call x1, Pallas kernels, on_device(): pl.pallas_call(kernel, out_shape=[jax.ShapeDtypeStruct((64, 256), F32), j...  57.3 us
    unnamed x5, local copies, waits for them, and re-layouts  3.13 us

profile of v2, /device:TPU:905, one launch (start us, length us, event | category | flops | bytes accessed | tf_op | source)
XLA Modules:
  0.0 61.1 jit_solution(5120439810291334132)
XLA Ops:
  0.6 1.0 %copy.8 = f32[1,1,1,256,1,1,256]{6,3,4,5,2,1,0:T(8,128)S(1)} copy(f32[1,1,1,256,1,1,256]{6,5,4,3,2,1,0:T(1,128)} %param.2) | data formatting | bytes 524288
  1.6 0.0 copy-start
  1.6 0.7 %copy-done = s32[1,1,2,1,1,2]{5,4,3,2,1,0:T(1,128)S(1)} copy-done((s32[1,1,2,1,1,2]{5,4,3,2,1,0:T(1,128)S(1)}, s32[1,1,2,1,1,2]{5,4,3,2,1,0:T(1,128)}, u32[]{:S(2)}) %copy-start) | copy-done | bytes 40
  2.3 57.3 %panels.1 = (f32[64,256]{1,0:T(8,128)S(1)}, f32[2,256,256]{2,1,0:T(8,128)S(1)}) custom-call(s32[2,2]{1,0:T(2,128)S(1)} %bitcast.11, f32[1,256,256]{2,1,0:T(8,128)S(1)} %bitcast.8), custom_call_target="tpu_custom_call" | custom-call | tf_op jit(solution)/shard_map/panels/pallas_call | solution.py:601
  59.6 0.7 %copy.4 = f32[1,1,1,64,1,1,256]{6,5,4,3,2,1,0:T(1,128)} copy(f32[1,1,1,64,1,1,256]{6,3,5,4,2,1,0:T(8,128)S(1)} %bitcast.10) | data formatting | bytes 131072
  60.3 0.8 %copy.10 = f32[2,1,1,256,256]{4,3,2,1,0:T(8,128)} copy(f32[2,1,1,256,256]{4,3,2,1,0:T(8,128)S(1)} %bitcast.9) | data formatting | bytes 1048576
Async XLA Ops:
  1.6 0.7 %copy-start = (s32[1,1,2,1,1,2]{5,4,3,2,1,0:T(1,128)S(1)}, s32[1,1,2,1,1,2]{5,4,3,2,1,0:T(1,128)}, u32[]{:S(2)}) copy-start(s32[1,1,2,1,1,2]{5,4,3,2,1,0:T(1,128)} %param.3) | copy-start | bytes 52

commit v3 on v2

--- a/solution.py
+++ b/solution.py
@@ -26,7 +26,7 @@
     return jnp.broadcast_to(x[k : k + 1, :], (8, 128))
 
 
-def factor_tile(tile):
+def factor_tile(tile, side=()):
     lane=lax.broadcasted_iota(jnp.int32,(8,128),1); sub=lax.broadcasted_iota(jnp.int32,(8,128),0)
     X=[tile[8*g:8*g+8,:] for g in range(16)]; FT=[];G=[]
     for b in range(0,16,2):
@@ -69,6 +69,8 @@
         for h,(Y,Z) in enumerate(((Y0,Z0),(Y1,Z1))):
             rs=lax.rsqrt(dv[h])
             FT.append(jnp.where(lane>=base+8*h+sub,Y*rs,0.0)); G.append(Z*rs)
+        if b//2 < len(side):
+            side[b//2]()
         if b<14:
             V0=jnp.where(lane<base+16,Z0,Y0); V1=jnp.where(lane<base+16,Z1,Y1)
             inb=(lane>=base)&(lane<base+16)
@@ -92,11 +94,10 @@
                         K0=K0-col*pv[0]*kr
                     else:
                         K0=K0-jnp.where(sub<q,c0[j]*pv[0],0.0)*rows(K0,q)
-                Kr=[rows(K0,j) for j in range(8)]+[rows(K1,j) for j in range(8)]
+                parts=([jnp.zeros((base,128),F32)] if base else [])+[K0,K1,jnp.zeros((112-base,128),F32)]
+                upd=dot(jnp.concatenate(X[b+4:],axis=0),jnp.concatenate(parts,axis=0))
                 for g in range(b+4,16):
-                    acc=jnp.where(inb,0.0,X[g])
-                    for j in range(16): acc=acc-lanes(X[g],base+j)*Kr[j]
-                    X[g]=acc
+                    X[g]=jnp.where(inb,0.0,X[g])-upd[8*(g-b-4):8*(g-b-4)+8]
     return jnp.concatenate(FT,axis=0), jnp.concatenate(G,axis=0)
 
 
@@ -136,8 +137,8 @@
 
 
 def kernel(
-    pattern, part, schur, panels,
-    xin, din, slab, prow, qcol, lead, work,
+    pattern_hbm, part_hbm, schur, panels,
+    pattern, staged, part, stage_sem, xin, din, slab, prow, qcol, lead, work,
     ready_y, ready_z, ready_w, x_send, x_recv, d_send, d_recv, z_send, zn_send, z_recv, y_send, y_recv,
     zd_send, zd_recv, yd_send, yd_recv, gd_send, gd_recv, g_send, g_recv,
     w_send, w_recv, wq_send, wq_recv,
@@ -157,6 +158,12 @@
             src_ref=src, dst_ref=dst, send_sem=send, recv_sem=recv, device_id=device, device_id_type=MESH
         )
 
+    loads = [
+        pltpu.make_async_copy(part_hbm, staged, stage_sem.at[0]),
+        pltpu.make_async_copy(pattern_hbm, pattern, stage_sem.at[1]),
+    ]
+    for load in loads:
+        load.start()
     barrier = pltpu.get_barrier_semaphore()
 
     def greet(device):
@@ -193,6 +200,10 @@
     count = 3
     for flag in served_y + served_z + [core == 0]:
         count = count + jnp.where(flag, 1, 0)
+    for load in loads:
+        load.wait()
+    for h in range(2):
+        part[0, :, 128 * h : 128 * h + 128] = staged[pl.ds(h, 256, stride=2), :]
     pl.semaphore_wait(barrier, count)
 
     def ready(sem, device):
@@ -308,6 +319,9 @@
 
     add_slab()
 
+    def g_copies(ref, j):
+        return [remote(ref, ref, g_send.at[j, i], g_recv.at[j, i], (peers[i], r, c)) for i in range(3)]
+
     def z_copies(k):
         return {
             sender: [
@@ -345,6 +359,8 @@
         @pl.when(far_row & (c == k))
         def _():
             prow[k, l] = slab[...]
+            for copy in g_copies(prow.at[k, l], k):
+                copy.start()
 
     for k in (1, 0):
         for sender, cols in TREE[k].items():
@@ -368,9 +384,6 @@
                     zd_copies(p, owner)[0].wait_recv()
                     row_sends(p, owner)
 
-    def g_copies(ref, j):
-        return [remote(ref, ref, g_send.at[j, i], g_recv.at[j, i], (peers[i], r, c)) for i in range(3)]
-
     def gather_panels():
         @pl.when(far_row)
         def _():
@@ -383,8 +396,10 @@
                 def _():
                     z_copies(k)[k][0].wait_recv()
 
-                for copy in g_copies(prow.at[k, l], k):
-                    copy.start()
+                @pl.when(c != k)
+                def _():
+                    for copy in g_copies(prow.at[k, l], k):
+                        copy.start()
 
         for k in range(2):
             @pl.when((c > 0) & (core == k))
@@ -468,69 +483,105 @@
         pl.semaphore_wait(ready_w, 1)
 
     gather_panels()
-    gather_lead(SECOND)
-    gather_lead(THIRD)
-    for p in FIRST:
+    for p in (SECOND, 0, THIRD, 1, 2):
         gather_lead(p)
 
+    def stack(a, b):
+        return jnp.concatenate([a, b], axis=0)
+
     zero = jnp.zeros((128, 128), F32)
-
-    def finish(upper0, g0, second, ref):
-        low = dot_t(second[:, :128], g0)
-        upper1, g1 = factor_tile(second[:, 128:] - dot_t(low, low))
-        ref[0, 0:128, 0:128] = upper0.T
-        ref[0, 0:128, 128:256] = zero
-        ref[0, 128:256, 0:128] = low
-        ref[0, 128:256, 128:256] = upper1.T
-        ref[1, 0:128, 0:128] = g0
-        ref[1, 0:128, 128:256] = zero
-        ref[1, 128:256, 0:128] = -dot(g1, dot(low, g0))
-        ref[1, 128:256, 128:256] = g1
-
     for owner in OWNERS[0]:
         lead_pass(0, owner)
     for owner in OWNERS[0]:
         lead_wait(0, owner)
-    upper0, g0 = factor_tile(lead[0, 0:128, 0:128])
+    up0, g0 = factor_tile(lead[0, 0:128, 0:128])
     for p in (1, 2):
         for owner in OWNERS[0]:
             lead_pass(p, owner)
     for p in (SECOND, THIRD):
         for owner in OWNERS[1]:
             lead_pass(p, owner)
+    panels_pass()
     for p in (1, 2):
         for owner in OWNERS[0]:
             lead_wait(p, owner)
-    finish(upper0, g0, lead[0, 128:256, :], work)
-    panels_pass()
     for p in (SECOND, THIRD):
         for owner in OWNERS[1]:
             lead_wait(p, owner)
-    inv0 = work[1]
-    l10 = dot_t(lead[1], inv0)
-    rest = lead[2] - dot_t(l10, l10)
-    work[2] = l10
+    low = dot_t(lead[0, 128:256, 0:128], g0)
+
+    def a1():
+        work[0, :, 0:128] = dot_t(lead[1, :, 0:128], g0)
+
+    def a2():
+        work[5, :, 0:128] = lead[1, :, 128:256] - dot_t(work[0, :, 0:128], low)
+
+    def a3():
+        top = work[0, 0:128, 0:128]
+        work[1, 0:128, 0:128] = lead[2, 0:128, 0:128] - dot_t(top, top)
+
+    def a4():
+        work[1, 128:256] = lead[2, 128:256] - dot_t(work[0, 128:256, 0:128], work[0, :, 0:128])
+
+    up1, g1 = factor_tile(lead[0, 128:256, 128:256] - dot_t(low, low), (a1, a2, a3, a4))
+    l10b = dot_t(work[5, :, 0:128], g1)
+    work[0, :, 128:256] = l10b
+    d22 = work[1, 0:128, 0:128] - dot_t(l10b[0:128], l10b[0:128])
     panels_wait()
-    l0 = jnp.where(r == 0, work[0], jnp.where(r == 1, work[2], dot_t(prow[0].reshape(256, 256), work[1])))
-    panels[0] = l0
-    panels[1] = prow[1].reshape(256, 256) - dot_t(l0, work[2])
-    work[5] = dot(work[1], qcol[0].reshape(256, 256))
-    work[6] = qcol[1].reshape(256, 256) - dot(work[2], work[5])
-
-    upper0, g0 = factor_tile(rest[:128, :128])
-    finish(upper0, g0, rest[128:, :], work.at[3:5])
-
-    inv1 = work[4]
-    panels[1] = jnp.where(r == 0, 0.0, jnp.where(r == 1, work[3], dot_t(panels[1], inv1)))
-    u1 = jnp.where(c < 2, 0.0, dot(inv1, work[6]))
-    u0 = jnp.where(c == 0, 0.0, work[5])
-    mine = pl.ds(pl.multiple_of(l * 64, 64), 64)
-    product = dot(panels[0, mine, :], u0) + dot(panels[1, mine, :], u1)
+
+    def b0():
+        work[1, 128:256] = work[1, 128:256] - dot_t(work[0, 128:256, 128:256], work[0, :, 128:256])
+
+    def b1():
+        x = dot_t(prow[0].reshape(256, 256)[:, 0:128], g0)
+        panels[0, :, 0:128] = jnp.where(r == 0, stack(up0.T, low), jnp.where(r == 1, work[0, :, 0:128], x))
+        work[3, 0:128] = dot(g0, qcol[0].reshape(256, 256)[0:128])
+
+    def b2():
+        work[5, :, 0:128] = prow[0].reshape(256, 256)[:, 128:256] - dot_t(panels[0, :, 0:128], low)
+        work[6, 0:128] = qcol[0].reshape(256, 256)[128:256] - dot(low, work[3, 0:128])
+
+    def b3():
+        x = dot_t(work[5, :, 0:128], g1)
+        panels[0, :, 128:256] = jnp.where(r == 0, stack(zero, up1.T), jnp.where(r == 1, work[0, :, 128:256], x))
+        work[3, 128:256] = dot(g1, work[6, 0:128])
+
+    def b4():
+        work[2] = prow[1].reshape(256, 256) - dot_t(panels[0], work[0])
+
+    def b5():
+        work[4] = qcol[1].reshape(256, 256) - dot(work[0], work[3])
+
+    up2, g2 = factor_tile(d22, (b0, b1, b2, b3, b4, b5))
+    low1 = dot_t(work[1, 128:256, 0:128], g2)
     half = lax.div(l, 2)
     lane = lax.broadcasted_iota(jnp.int32, (64, 256), 1)
     flag = jnp.where(lane < 128, pattern[half, 0], pattern[half, 1])
     keep = (flag > 0) | (r < 2) | (c < 2)
-    schur[...] = slab[...] - jnp.where(keep, product, 0.0)
+
+    def c1():
+        x = dot_t(work[2, :, 0:128], g2)
+        work[5, :, 0:128] = x
+        panels[1, :, 0:128] = jnp.where(r == 0, 0.0, jnp.where(r == 1, stack(up2.T, low1), x))
+        work[6, 0:128] = dot(g2, work[4, 0:128])
+
+    def c2():
+        work[5, :, 128:256] = work[2, :, 128:256] - dot_t(work[5, :, 0:128], low1)
+        work[6, 128:256] = work[4, 128:256] - dot(low1, work[6, 0:128])
+
+    def c3():
+        u0 = jnp.where(c == 0, 0.0, work[3])
+        u1 = jnp.where(c < 2, 0.0, work[6, 0:128])
+        product = dot(panels[0, own_rows, :], u0) + dot(panels[1, own_rows, 0:128], u1)
+        work[4, 0:64] = slab[...] - jnp.where(keep, product, 0.0)
+
+    up3, g3 = factor_tile(work[1, 128:256, 128:256] - dot_t(low1, low1), (c1, c2, c3))
+    x = dot_t(work[5, :, 128:256], g3)
+    panels[1, :, 128:256] = jnp.where(r == 0, 0.0, jnp.where(r == 1, stack(zero, up3.T), x))
+    u1 = jnp.where(c < 2, 0.0, dot(g3, work[6, 128:256]))
+    result = work[4, 0:64] - jnp.where(keep, dot(panels[1, own_rows, 128:256], u1), 0.0)
+    for h in range(2):
+        schur[pl.ds(h, 64, stride=2), :] = result[:, 128 * h : 128 * h + 128]
 
     for i in range(3):
         x_copy(i).wait_send()
@@ -601,12 +652,13 @@
     schur, panels = pl.pallas_call(
         kernel,
         out_shape=[
-            jax.ShapeDtypeStruct((64, 256), F32),
+            jax.ShapeDtypeStruct((128, 128), F32),
             jax.ShapeDtypeStruct((2, 256, 256), F32),
         ],
-        in_specs=[pl.BlockSpec(memory_space=pltpu.SMEM), vmem],
+        in_specs=[pl.BlockSpec(memory_space=pl.ANY)] * 2,
         out_specs=[vmem] * 2,
         scratch_shapes=[
+            pltpu.SMEM((2, 2), jnp.int32), pltpu.VMEM((512, 128), F32), pltpu.VMEM((1, 256, 256), F32), dma((2,)),
             pltpu.VMEM((4, 64, 256), F32), pltpu.VMEM((4, 1, 256, 256), F32), pltpu.VMEM((64, 256), F32),
             pltpu.VMEM((2, 4, 64, 256), F32), pltpu.VMEM((2, 4, 64, 256), F32), pltpu.VMEM((3, 256, 256), F32),
             pltpu.VMEM((7, 256, 256), F32),
@@ -619,7 +671,7 @@
             collective_id=0, has_side_effects=True, vmem_limit_bytes=32 * 1024 * 1024
         ),
         name="panels",
-    )(pattern.reshape(2, 2), partials.reshape(1, 256, 256))
+    )(pattern.reshape(2, 2), partials.reshape(512, 128))
     return schur.reshape(1, 1, 1, 64, 1, 1, 256), panels.reshape(2, 1, 1, 256, 256)
 
 

time: 61.3 us -> 56 us (0.914)
  the two profiles are of different devices: /device:TPU:905 before, /device:TPU:736 now
where the time goes in v3:
time: 56 us; the launch traced here: 55.8 us
  Pallas kernels  52.1 us (93%)
  local copies, waits for them, and re-layouts  3.05 us (5%)
  between operations  0.65 us (1%)
    pallas_call x1, Pallas kernels, on_device(): pl.pallas_call(kernel, out_shape=[jax.ShapeDtypeStruct((128, 128), F32),...  52.1 us
    unnamed x6, local copies, waits for them, and re-layouts  3.05 us

profile of v3, /device:TPU:736, one launch (start us, length us, event | category | flops | bytes accessed | tf_op | source)
XLA Modules:
  0.0 55.8 jit_solution(17484238000969655987)
XLA Ops:
  0.6 0.0 copy-start.1
  0.6 0.7 %copy-done.1 = s32[1,1,2,1,1,2]{5,4,3,2,1,0:T(1,128)S(1)} copy-done((s32[1,1,2,1,1,2]{5,4,3,2,1,0:T(1,128)S(1)}, s32[1,1,2,1,1,2]{5,4,3,2,1,0:T(1,128)}, u32[]{:S(2)}) %copy-start.1) | copy-done | bytes 40
  1.3 0.0 copy-start
  1.3 0.9 %copy-done = f32[1,1,1,256,1,1,256]{6,5,4,3,2,1,0:T(1,128)S(1)} copy-done((f32[1,1,1,256,1,1,256]{6,5,4,3,2,1,0:T(1,128)S(1)}, f32[1,1,1,256,1,1,256]{6,5,4,3,2,1,0:T(1,128)}, u32[]{:S(2)}) %copy-start) | copy-done | bytes 262168
  2.3 52.1 %panels.1 = (f32[128,128]{1,0:T(8,128)S(1)}, f32[2,256,256]{2,1,0:T(8,128)S(1)}) custom-call(s32[2,2]{1,0:T(2,128)S(1)} %bitcast.9, f32[512,128]{1,0:T(8,128)S(1)} %bitcast.7), custom_call_target="tpu_custom_call" | custom-call | tf_op jit(solution)/shard_map/panels/pallas_call | solution.py:652
  54.3 0.6 %copy.8 = f32[1,1,1,64,1,1,256]{6,5,4,3,2,1,0:T(1,128)} copy(f32[1,1,1,64,1,1,256]{6,5,4,3,2,1,0:T(1,128)S(1)} %bitcast.8) | data formatting | bytes 131072
  55.0 0.8 %copy.9 = f32[2,1,1,256,256]{4,3,2,1,0:T(8,128)} copy(f32[2,1,1,256,256]{4,3,2,1,0:T(8,128)S(1)} %bitcast.6) | data formatting | bytes 1048576
Async XLA Ops:
  0.6 0.7 %copy-start.1 = (s32[1,1,2,1,1,2]{5,4,3,2,1,0:T(1,128)S(1)}, s32[1,1,2,1,1,2]{5,4,3,2,1,0:T(1,128)}, u32[]{:S(2)}) copy-start(s32[1,1,2,1,1,2]{5,4,3,2,1,0:T(1,128)} %param.3) | copy-start | bytes 52
  1.3 0.9 %copy-start = (f32[1,1,1,256,1,1,256]{6,5,4,3,2,1,0:T(1,128)S(1)}, f32[1,1,1,256,1,1,256]{6,5,4,3,2,1,0:T(1,128)}, u32[]{:S(2)}) copy-start(f32[1,1,1,256,1,1,256]{6,5,4,3,2,1,0:T(1,128)} %param.2) | copy-start | bytes 786436

commit v4 on v3

--- a/solution.py
+++ b/solution.py
@@ -102,7 +102,7 @@
 
 
 TREE = (
-    {0: (1, 2, 5, 8, 15, 13), 2: (3, 4), 5: (6, 7), 8: (9, 10), 15: (14,), 13: (12, 11)},
+    {0: (1, 2, 5, 8, 11, 12, 13, 14, 15), 2: (3, 4), 5: (6, 7), 8: (9, 10)},
     {1: (0, 2, 3, 6, 9, 14, 12), 3: (4, 5), 6: (7, 8), 9: (10,), 14: (15, 13), 12: (11,)},
 )
 COL_ORDER = (tuple(range(1, 16)), (0,) + tuple(range(2, 16)))
@@ -655,7 +655,7 @@
             jax.ShapeDtypeStruct((128, 128), F32),
             jax.ShapeDtypeStruct((2, 256, 256), F32),
         ],
-        in_specs=[pl.BlockSpec(memory_space=pl.ANY)] * 2,
+        in_specs=[pl.BlockSpec(memory_space=pltpu.HBM)] * 2,
         out_specs=[vmem] * 2,
         scratch_shapes=[
             pltpu.SMEM((2, 2), jnp.int32), pltpu.VMEM((512, 128), F32), pltpu.VMEM((1, 256, 256), F32), dma((2,)),
@@ -663,7 +663,7 @@
             pltpu.VMEM((2, 4, 64, 256), F32), pltpu.VMEM((2, 4, 64, 256), F32), pltpu.VMEM((3, 256, 256), F32),
             pltpu.VMEM((7, 256, 256), F32),
             regular, regular((16,)), regular,
-            dma((3,)), dma((3,)), dma((3, 3)), dma((3, 4)), dma((7,)), dma((2,)), dma((2,)), dma((7,)), dma,
+            dma((3,)), dma((3,)), dma((3, 3)), dma((3, 4)), dma((9,)), dma((2,)), dma((2,)), dma((7,)), dma,
             dma((5, 15)), dma((5,)), dma((5, 8)), dma((5,)), dma((5, 3)), dma((5, 4)), dma((3, 3)), dma((3, 3)),
             dma((5, 4)), dma((5, 4)), dma, dma,
         ],

time: 56 us -> 54.8 us (0.979)
  the two profiles are of different devices: /device:TPU:736 before, /device:TPU:992 now
where the time goes in v4:
time: 54.8 us; the launch traced here: 54.6 us
  Pallas kernels  50.9 us (93%)
  local copies, waits for them, and re-layouts  3.05 us (6%)
  between operations  0.65 us (1%)
    pallas_call x1, Pallas kernels, on_device(): pl.pallas_call(kernel, out_shape=[jax.ShapeDtypeStruct((128, 128), F32),...  50.9 us
    unnamed x6, local copies, waits for them, and re-layouts  3.05 us

profile of v4, /device:TPU:992, one launch (start us, length us, event | category | flops | bytes accessed | tf_op | source)
XLA Modules:
  0.0 54.6 jit_solution(3955249552094179055)
XLA Ops:
  0.6 0.0 copy-start.1
  0.6 0.7 %copy-done.1 = s32[1,1,2,1,1,2]{5,4,3,2,1,0:T(1,128)S(1)} copy-done((s32[1,1,2,1,1,2]{5,4,3,2,1,0:T(1,128)S(1)}, s32[1,1,2,1,1,2]{5,4,3,2,1,0:T(1,128)}, u32[]{:S(2)}) %copy-start.1) | copy-done | bytes 40
  1.3 0.0 copy-start
  1.3 0.9 %copy-done = f32[1,1,1,256,1,1,256]{6,5,4,3,2,1,0:T(1,128)S(1)} copy-done((f32[1,1,1,256,1,1,256]{6,5,4,3,2,1,0:T(1,128)S(1)}, f32[1,1,1,256,1,1,256]{6,5,4,3,2,1,0:T(1,128)}, u32[]{:S(2)}) %copy-start) | copy-done | bytes 262168
  2.3 50.9 %panels.1 = (f32[128,128]{1,0:T(8,128)S(1)}, f32[2,256,256]{2,1,0:T(8,128)S(1)}) custom-call(s32[2,2]{1,0:T(2,128)S(1)} %bitcast.9, f32[512,128]{1,0:T(8,128)S(1)} %bitcast.7), custom_call_target="tpu_custom_call" | custom-call | tf_op jit(solution)/shard_map/panels/pallas_call | solution.py:652
  53.2 0.6 %copy.8 = f32[1,1,1,64,1,1,256]{6,5,4,3,2,1,0:T(1,128)} copy(f32[1,1,1,64,1,1,256]{6,5,4,3,2,1,0:T(1,128)S(1)} %bitcast.8) | data formatting | bytes 131072
  53.8 0.8 %copy.9 = f32[2,1,1,256,256]{4,3,2,1,0:T(8,128)} copy(f32[2,1,1,256,256]{4,3,2,1,0:T(8,128)S(1)} %bitcast.6) | data formatting | bytes 1048576
Async XLA Ops:
  0.6 0.7 %copy-start.1 = (s32[1,1,2,1,1,2]{5,4,3,2,1,0:T(1,128)S(1)}, s32[1,1,2,1,1,2]{5,4,3,2,1,0:T(1,128)}, u32[]{:S(2)}) copy-start(s32[1,1,2,1,1,2]{5,4,3,2,1,0:T(1,128)} %param.3) | copy-start | bytes 52
  1.3 0.9 %copy-start = (f32[1,1,1,256,1,1,256]{6,5,4,3,2,1,0:T(1,128)S(1)}, f32[1,1,1,256,1,1,256]{6,5,4,3,2,1,0:T(1,128)}, u32[]{:S(2)}) copy-start(f32[1,1,1,256,1,1,256]{6,5,4,3,2,1,0:T(1,128)} %param.2) | copy-start | bytes 786436
